TPU v7x, 1024 devices: a whole 4x8x16 slice. The times are simulated.
1024 devices in a mesh: dp: 16 (over y_hi, x), expert: 32 (over z, core), pair: 2 (over y_lo).
Axes of the slice: x: 4, y: 8 (y_hi: 4, y_lo: 2; y = y_hi * 2 + y_lo), z: 16, core: 2. Of those that a mesh axis runs over, the one named last changes fastest.
Arguments:
- tokens: bfloat16 [1024, 7168], P('expert', 'pair'), may hold values from -6 to 6
- routes: int32 [1024, 8], P('expert'), may hold values from 0 to 31, all different within a row; in each aligned block of 32 rows (0 to 31, 32 to 63, ...) at most 16 rows name the same one
- gates: float32 [1024, 8], P('expert'), may hold values from 0.05 to 0.6
- w_gate: bfloat16 [32, 7168, 2048], P('expert', 'pair', 'dp'), may hold values from -0.0625 to 0.0625
- w_up: bfloat16 [32, 7168, 2048], P('expert', 'pair', 'dp'), may hold values from -0.0625 to 0.0625
- w_down: bfloat16 [32, 2048, 7168], P('expert', 'dp', 'pair'), may hold values from -0.125 to 0.125
Outputs:
- mixed: bfloat16 [1024, 7168], P('expert', 'pair')
Inputs may be any that keep to these rules, and one draw needn't show every extreme that they name: `routes`: each row names 8 different experts. Among the rows of one device's block of 32 tokens no expert is named more than 16 times, and in every draw some expert is named exactly 16 times in some block.
All inputs are finite; a program needn't handle non-finite values.
Results may differ from a plain program's by a relative error of at most 0.03.
Values may be sent and summed in bfloat16 or wider, within the bound.
A program may use at most 32 MiB of HBM per device.

v0:
```python
import jax
import jax.numpy as jnp
from jax import lax
from jax.sharding import PartitionSpec as P

EXPERTS = 32
CAP = 16


def per_device(tokens, routes, gates, w_gate, w_up, w_down):
    tok_rows, half_width = tokens.shape
    top_count = routes.shape[1]
    local_count = w_gate.shape[0]
    experts = EXPERTS
    capacity = CAP
    groups = lax.axis_size("dp")
    owners = lax.axis_size("expert")
    share_width = half_width // groups
    levels = capacity // groups
    group_index = lax.axis_index("dp")
    expert_ids = jnp.arange(experts, dtype=jnp.int32)
    onehot = (routes.reshape(tok_rows * top_count)[:, None] == expert_ids[None, :]).astype(
        jnp.int32
    )
    before = jnp.cumsum(onehot, axis=0) - onehot
    slot_index = jnp.sum(before * onehot, axis=1)
    expert_hot = onehot.astype(jnp.float32).reshape(tok_rows, top_count, experts)
    slot_hot = (slot_index[:, None] == jnp.arange(capacity, dtype=jnp.int32)[None, :]).astype(
        jnp.float32
    )
    slot_hot = slot_hot.reshape(tok_rows, top_count, capacity)
    placing = jnp.einsum("tke,tkc->cet", expert_hot, slot_hot).astype(jnp.bfloat16)
    columns = lax.dynamic_slice_in_dim(tokens, group_index * share_width, share_width, 1)
    outgoing = jnp.dot(
        placing.reshape(capacity * experts, tok_rows), columns, preferred_element_type=jnp.float32
    ).astype(jnp.bfloat16)
    outgoing = outgoing.reshape(capacity, experts, share_width)
    arrived = lax.all_to_all(outgoing, "expert", split_axis=1, concat_axis=1, tiled=True)
    slot_count = arrived.shape[0]
    width = arrived.shape[2]
    shaped = arrived.reshape(slot_count, owners, local_count, width)
    arrived = jnp.transpose(shaped, (2, 0, 1, 3)).reshape(local_count, slot_count * owners, width)
    part_block = lax.all_gather(arrived, "dp", axis=2, tiled=True)
    gate_part = jnp.einsum("jrd,jdf->jrf", part_block, w_gate, preferred_element_type=jnp.float32)
    up_part = jnp.einsum("jrd,jdf->jrf", part_block, w_up, preferred_element_type=jnp.float32)
    gate_sum = gate_part
    up_sum = up_part
    gate_sum, up_sum = (
        lax.psum(gate_sum.astype(jnp.bfloat16), "pair").astype(jnp.float32),
        lax.psum(up_sum.astype(jnp.bfloat16), "pair").astype(jnp.float32),
    )
    hidden = (jax.nn.silu(gate_sum) * up_sum).astype(jnp.bfloat16)
    projected = jnp.einsum("jrf,jfd->rjd", hidden, w_down, preferred_element_type=jnp.float32)
    summed = lax.psum_scatter(
        projected.reshape(lax.axis_size("dp") * (levels * owners), local_count * half_width).astype(
            jnp.bfloat16
        ),
        "dp",
        scatter_dimension=0,
        tiled=True,
    )
    results = summed.reshape(levels, experts, half_width)
    returned = lax.all_to_all(results, "expert", split_axis=1, concat_axis=1, tiled=True)
    level_ids = group_index * levels + jnp.arange(levels, dtype=jnp.int32)
    level_hot = (
        (slot_index[:, None] == level_ids[None, :])
        .astype(jnp.float32)
        .reshape(tok_rows, top_count, levels)
    )
    weighted = gates[:, :, None] * expert_hot
    mixing = jnp.einsum("tke,tkc->tce", weighted, level_hot, precision=lax.Precision.HIGHEST)
    partial_value = jnp.dot(
        mixing.reshape(tok_rows, levels * experts),
        returned.reshape(levels * experts, half_width).astype(jnp.float32),
        precision=lax.Precision.HIGHEST,
    )
    summed_out = lax.psum(partial_value.astype(jnp.bfloat16), "dp")
    return summed_out


def solution(mesh):
    placed = (
        P("expert", "pair"),
        P("expert", None),
        P("expert", None),
        P("expert", "pair", "dp"),
        P("expert", "pair", "dp"),
        P("expert", "dp", "pair"),
    )
    return jax.shard_map(
        per_device, mesh=mesh, in_specs=placed, out_specs=P("expert", "pair"), check_vma=False
    )
```

profile of v0, /device:TPU:30, one launch (start us, length us, event | category | flops | bytes accessed | tf_op | source)
XLA Modules:
  0.0 518.7 jit_solution(1887758997081827710)
XLA Ops:
  6.5 0.9 copy.25
  7.6 0.6 reduce-window.6
  8.2 0.2 slice_reduce_fusion
  8.6 0.4 fusion.16
  9.2 1.1 convolution_convert_fusion.2
  10.6 41.7 %all_to_all.10 = bf16[16,32,224]{2,0,1:T(8,128)(2,1)S(1)} all-to-all(bf16[16,32,224]{2,0,1:T(8,128)(2,1)S(1)} %copy.31), channel_id=1, replica_groups=mesh['dp'=16,'expert'=32,'pair'=2] {'expert'}, dimensions={1} | all-to-all | bytes 458752 | tf_op jit(solution)/shard_map/all_to_all | solution.py:38
  52.4 0.8 copy.33
  53.3 78.2 %all-gather.2.cloned.1.call-done = bf16[1,512,3584]{1,2,0:T(8,128)(2,1)} async-done(((bf16[1,512,224]{1,2,0:T(8,128)(2,1)}), bf16[1,512,3584]{1,2,0:T(8,128)(2,1)}) %all-gather.2.cloned.1.call-update) | async-done | bytes 3670032 | tf_op jit(solution)/shard_map/all_gather | solution.py:43
  131.5 4.0 fusion.10
  135.5 1.8 fusion.13
  137.4 49.7 %all-reduce.6.cloned.1.call-done = (bf16[1,512,128]{2,1,0:T(8,128)(2,1)}, bf16[1,512,128]{2,1,0:T(8,128)(2,1)}) async-done(((bf16[1,512,128]{2,1,0:T(8,128)(2,1)}, bf16[1,512,128]{2,1,0:T(8,128)(2,1)}), (bf16[1,512,128]{2,1,0:T(8,128)(2,1)}, bf16[1,512,128]{2,1,0:T(8,128)(2,1)})) %all-reduce.6.cloned.1.call-update) | async-done | bytes 262160 | tf_op jit(solution)/shard_map/psum | solution.py:50
  187.1 3.9 convolution_convert_fusion
  191.0 111.9 %reduce-scatter.2.cloned.1.call-done = bf16[32,3584]{1,0:T(8,128)(2,1)} async-done(((bf16[512,3584]{1,0:T(8,128)(2,1)}), bf16[32,3584]{1,0:T(8,128)(2,1)}) %reduce-scatter.2.cloned.1.call-update) | async-done | bytes 229392 | tf_op jit(solution)/shard_map/reduce_scatter | solution.py:54
  302.9 1.3 copy.47
  304.2 0.5 broadcast.40
  304.7 2.0 reduce.2
  306.7 0.7 reshape.96
  307.4 13.3 %all-to-all-start.1 = ((bf16[32,2,1792]{2,1,0:T(2,128)(2,1)}), bf16[32,2,1792]{2,1,0:T(2,128)(2,1)S(1)}, u32[]{:S(2)}, u32[]{:S(2)}) async-start(bf16[32,2,1792]{2,1,0:T(2,128)(2,1)} %reshape.96), calls=%async_computation.2 | async-start | bytes 458752 | tf_op jit(solution)/shard_map/all_to_all | solution.py:63
  320.8 0.3 fusion.29
  321.2 20.9 %all-to-all-done.1 = bf16[32,2,1792]{2,1,0:T(2,128)(2,1)S(1)} async-done(((bf16[32,2,1792]{2,1,0:T(2,128)(2,1)}), bf16[32,2,1792]{2,1,0:T(2,128)(2,1)S(1)}, u32[]{:S(2)}, u32[]{:S(2)}) %all-to-all-start.1) | async-done | bytes 229408 | tf_op jit(solution)/shard_map/all_to_all | solution.py:63
  342.1 0.2 reshape.97
  342.2 1.0 convolution_convert_fusion.1
  343.3 167.3 %all-reduce.4.cloned.1.call-done = bf16[32,3584]{1,0:T(8,128)(2,1)} async-done(((bf16[32,3584]{1,0:T(8,128)(2,1)}), bf16[32,3584]{1,0:T(8,128)(2,1)}) %all-reduce.4.cloned.1.call-update) | async-done | bytes 229392 | tf_op jit(solution)/shard_map/psum | solution.py:77
  510.6 1.6 copy.52
  (31 shorter events, 1.2 us)
Async XLA Ops:
  6.5 180.5 %copy-start = (bf16[1,128,3584]{2,1,0:T(8,128)(2,1)S(1)}, bf16[1,128,3584]{2,1,0:T(8,128)(2,1)}, u32[]{:S(2)}) copy-start(bf16[1,128,3584]{2,1,0:T(8,128)(2,1)} %param.11) | copy-start | bytes 2752516
  6.5 124.9 %copy-start.2 = (bf16[1,3584,128]{2,1,0:T(8,128)(2,1)S(1)}, bf16[1,3584,128]{2,1,0:T(8,128)(2,1)}, u32[]{:S(2)}) copy-start(bf16[1,3584,128]{2,1,0:T(8,128)(2,1)} %param.10) | copy-start | bytes 2752516
  6.5 124.9 %all-gather.2.cloned.1.call-start = ((), (), s32[]{:S(2)}) async-start(), calls=%async_computation.3 | async-start | bytes 3899392 | tf_op jit(solution)/shard_map/all_gather | solution.py:43
  10.3 125.2 %copy-start.3 = (bf16[1,3584,128]{2,1,0:T(8,128)(2,1)S(1)}, bf16[1,3584,128]{2,1,0:T(8,128)(2,1)}, u32[]{:S(2)}) copy-start(bf16[1,3584,128]{2,1,0:T(8,128)(2,1)} %param.9) | copy-start | bytes 2752516
  53.2 133.8 %all-reduce.6.cloned.1.call-start = ((), (), s32[]{:S(2)}) async-start(), calls=%async_computation.6 | async-start | bytes 524288 | tf_op jit(solution)/shard_map/psum | solution.py:50
  131.5 4.0 copy-start.1
  137.3 165.6 %reduce-scatter.2.cloned.1.call-start = ((), (), s32[]{:S(2)}) async-start(), calls=%async_computation.4 | async-start | bytes 3899392 | tf_op jit(solution)/shard_map/reduce_scatter | solution.py:54
  190.9 129.8 %copy-start.4 = (f32[32,8]{0,1:T(8,128)S(1)}, f32[32,8]{0,1:T(8,128)}, u32[]{:S(2)}) copy-start(f32[32,8]{0,1:T(8,128)} %param.8) | copy-start | bytes 3076
  307.4 34.7 %all-to-all-start.1 = ((bf16[32,2,1792]{2,1,0:T(2,128)(2,1)}), bf16[32,2,1792]{2,1,0:T(2,128)(2,1)S(1)}, u32[]{:S(2)}, u32[]{:S(2)}) async-start(bf16[32,2,1792]{2,1,0:T(2,128)(2,1)} %reshape.96), calls=%async_computation.2 | async-start | bytes 458752 | tf_op jit(solution)/shard_map/all_to_all | solution.py:63
  320.7 189.9 %all-reduce.4.cloned.1.call-start = ((), (), s32[]{:S(2)}) async-start(), calls=%async_computation.5 | async-start | bytes 458752 | tf_op jit(solution)/shard_map/psum | solution.py:77
Sparse Core Ops, SparseCore 0:
  53.3 78.0 all-gather.1
  137.4 49.5 all-reduce.5
  193.3 109.4 reduce-scatter.1
  343.4 167.1 all-reduce.3
where the time goes:
time: 519 us
  waiting for transfers between devices  428 us (82%)
  blocking collectives  41.7 us (8%)
  starting transfers between devices  13.4 us (3%)
  between operations  13.2 us (3%)
  matrix products  12.5 us (2%)
  local copies, waits for them, and re-layouts  7.13 us (1%)
    psum x1, waiting for transfers between devices, per_device(): summed_out = lax.psum(partial_value.astype(jnp.bfloat16), 'dp')  167 us
    reduce_scatter x1, waiting for transfers between devices, per_device(): lax.psum_scatter(projected.reshape(lax.axis_size('dp') * (levels * owners...  112 us
    all_gather x1, waiting for transfers between devices, per_device(): part_block = lax.all_gather(arrived, 'dp', axis=2, tiled=True)  78.2 us
    psum x1, waiting for transfers between devices, per_device(): lax.psum(up_sum.astype(jnp.bfloat16), 'pair').astype(jnp.float32)  49.7 us
    all_to_all x1, blocking collectives, per_device(): lax.all_to_all(outgoing, 'expert', split_axis=1, concat_axis=1, tiled=True)  41.7 us
    all_to_all x1, waiting for transfers between devices, per_device(): lax.all_to_all(results, 'expert', split_axis=1, concat_axis=1, tiled=True)  20.9 us
    all_to_all x1, starting transfers between devices, per_device(): lax.all_to_all(results, 'expert', split_axis=1, concat_axis=1, tiled=True)  13.3 us
  transfers between devices with their start and end apart: 5, of which 5 were waited for; matrix products, arithmetic and copies ran while one was open for 0% of the time, Pallas kernels for 0%

commit v1 on v0

v1 whole, which is shorter than its diff:
```python
import jax
import jax.numpy as jnp
from jax import lax
from jax.experimental import pallas as pl
from jax.experimental.pallas import tpu as pltpu
from jax.sharding import PartitionSpec as P

MESH = pl.DeviceIdType.MESH
NX = 4
NY = 4
NZ = 16
NCORE = 2
BLOCK = 32
HALF = 3584
QUART = 896
SUB = 256
FFS = 128
CHUNKS = 8
PER = 2
CUT = 32
NB = 2
ROWS = PER * BLOCK
OFFSETS = (1, -1, 2, -2, 3, -3, 4, -4, 5, -5, 6, -6, 7, -7, 8, 0)
OWN = NZ - 1
JUMP = 2
TOPK = 8
ORDER = (('A', (0,)), ('A', (1,)), ('F', (0,)), ('A', (2,)), ('F', (1,)), ('A', (3,)), ('B', (0,)), ('F', (2,)), ('A', (4,)), ('B', (1,)), ('A', (5,)), ('F', (3,)), ('C', (0,)), ('B', (2,)), ('A', (6,)), ('F', (4,)), ('C', (1,)), ('A', (7,)), ('F', (5,)), ('B', (3,)), ('G', (0,)), ('C', (2,)), ('F', (6,)), ('B', (4,)), ('C', (3,)), ('G', (1,)), ('F', (7,)), ('B', (5,)), ('D', (0,)), ('C', (4,)), ('G', (2,)), ('B', (6,)), ('C', (5,)), ('G', (3,)), ('D', (1,)), ('E', (0,)), ('B', (7,)), ('C', (6,)), ('G', (4,)), ('D', (2,)), ('E', (1,)), ('G', (5,)), ('C', (7,)), ('D', (3,)), ('G', (6,)), ('E', (2,)), ('D', (4,)), ('D', (5,)), ('G', (7,)), ('E', (3,)), ('D', (6,)), ('E', (4,)), ('D', (7,)), ('E', (5,)), ('E', (6,)), ('E', (7,)))


def kernel(
    tok, routes, gates, wg, wu, wd, out,
    x_all, w_gu, w_d, meta, gu_own, gu_send, gu_recv, part, xr, ys, yr, zs, zr, fo,
    w_loc, w_send, w_recv, zg_send, zg_recv, mg_send, mg_recv, bg_send, bg_recv, xg_send, xg_recv,
    xf_send, xf_recv, yg_send, yg_recv,
    p_send, p_recv, xr_send, xr_recv, xc_send, xc_recv, yr_send, yr_recv, zr_send, zr_recv, ag_send, ag_recv,
):
    dp = lax.axis_index("dp")
    ex = lax.axis_index("expert")
    pr = lax.axis_index("pair")
    yh, x = dp // NX, lax.rem(dp, NX)
    z, core = ex // NCORE, lax.rem(ex, NCORE)

    def at_z(off):
        return {"expert": lax.rem(z + (off + NZ), NZ) * NCORE + core}

    def at_x(d):
        return {"dp": yh * NX + lax.rem(x + d, NX)}

    x1, x2, x3 = (lax.rem(x + d, NX) for d in (1, 2, 3))

    def at_y(d):
        return {"dp": lax.rem(yh + d, NY) * NX + x}

    def at_dp(d):
        return {"dp": lax.rem(dp + d, NX * NY)}

    sibling = {"expert": z * NCORE + (1 - core)}
    partner = {"pair": 1 - pr}

    def remote(src, dst, send, recv, where):
        return pltpu.make_async_remote_copy(
            src_ref=src, dst_ref=dst, send_sem=send, recv_sem=recv,
            device_id=where, device_id_type=MESH,
        )

    barrier = pltpu.get_barrier_semaphore()
    for k in range(NZ - 1):
        pl.semaphore_signal(barrier, inc=1, device_id=at_z(OFFSETS[k]), device_id_type=MESH)
    for d in range(1, NX * NY):
        pl.semaphore_signal(barrier, inc=1, device_id=at_dp(d), device_id_type=MESH)
    pl.semaphore_signal(barrier, inc=1, device_id=sibling, device_id_type=MESH)
    pl.semaphore_signal(barrier, inc=1, device_id=partner, device_id_type=MESH)

    wcol = pl.multiple_of(core * FFS, FFS)
    wcol_up = pl.multiple_of((NCORE + core) * FFS, FFS)
    w_dsts = (
        (wg.at[0], w_gu.at[:, pl.ds(wcol, FFS)]),
        (wu.at[0], w_gu.at[:, pl.ds(wcol_up, FFS)]),
        (wd.at[0], w_d.at[pl.ds(wcol, FFS)]),
    )
    local = [pltpu.make_async_copy(s, d, w_loc.at[i]) for i, (s, d) in enumerate(w_dsts)]
    own = slice(OWN * BLOCK, NZ * BLOCK)
    mine_in = pltpu.make_async_copy(tok, x_all.at[own], w_loc.at[3])
    mine_in.start()
    for cp in local:
        cp.start()

    lane = lax.broadcasted_iota(jnp.int32, (BLOCK, 128), 1)
    first = jnp.zeros((BLOCK, 128), jnp.float32)
    second = jnp.zeros((BLOCK, 128), jnp.float32)
    for k in range(TOPK):
        r = routes[:, k : k + 1]
        g = gates[:, k : k + 1]
        first = first + jnp.where(lane == r, g, 0.0)
        second = second + jnp.where(lane == r + 32, g, 0.0)
    low = second - second.astype(jnp.bfloat16).astype(jnp.float32)
    meta[own, :] = jnp.where(lane < 32, first, low).astype(jnp.bfloat16)
    ys[:, QUART:] = jnp.zeros((CHUNKS * ROWS, NY * SUB - QUART), jnp.bfloat16)

    mine_in.wait()
    pl.semaphore_wait(barrier, NZ - 1 + NX * NY - 1 + 2)

    nb = NB * 128
    na = QUART - nb
    qcol = pl.multiple_of(x * QUART, 128)
    acol = pl.ds(pl.multiple_of(x * na, 128), na)
    bcol = pl.ds(pl.multiple_of(NX * na + yh * nb, 128), nb) if nb else None
    pieces = [(meta, slice(None), mg_send, mg_recv), (x_all, acol, zg_send, zg_recv)]
    if nb:
        pieces.append((x_all, bcol, bg_send, bg_recv))
    sends = []
    zgot = {}

    def hop(src, k):
        step = OFFSETS[k] if src == OWN else (JUMP if OFFSETS[k] > 0 else -JUMP)
        cps = []
        for ref, cols, ssem, rsem in pieces:
            cp = remote(
                ref.at[pl.ds(src * BLOCK, BLOCK), cols], ref.at[pl.ds(k * BLOCK, BLOCK), cols],
                ssem.at[k], rsem.at[k], at_z(step),
            )
            cp.start()
            cps.append(cp)
        zgot[k] = cps
        sends.extend(cps)

    for k in range(2 * JUMP):
        hop(OWN, k)
    weights = [
        remote(s, d, w_send.at[i], w_recv.at[i], sibling) for i, (s, d) in enumerate(w_dsts)
    ]
    for cp in weights:
        cp.start()
    sends += weights

    gathered = {}
    halves = {}
    paired = {}
    xred = {}
    xcom = {}
    yred = {}
    zred = {}

    def stage_a(j):
        for k in range(PER * j, PER * j + PER):
            if k == OWN:
                continue
            for cp in zgot[k]:
                cp.wait_recv()
            if k + 2 * JUMP < OWN:
                hop(k, k + 2 * JUMP)
        count = ROWS - BLOCK if j == CHUNKS - 1 else ROWS
        rows = pl.ds(ROWS * j, count)
        where = x_all.at[rows, acol]
        cps = [
            remote(where, where, xg_send.at[j, d - 1], xg_recv.at[j, d - 1], at_x(d))
            for d in (1, 3)
        ]
        halves[j] = cps
        ycps = []
        if nb:
            where = x_all.at[rows, bcol]
            ycps = [
                remote(where, where, yg_send.at[j, d - 1], yg_recv.at[j, d - 1], at_y(d))
                for d in (2, 1, 3)
            ]
        for cp in cps + ycps:
            cp.start()
        gathered[j] = list(ycps)
        sends.extend(cps + ycps)

    def stage_f(j):
        count = ROWS - BLOCK if j == CHUNKS - 1 else ROWS
        cut = count // 2
        for i, (cp, d) in enumerate(zip(halves[j], (1, 3))):
            cp.wait_recv()
            low, size = (0, cut) if i == 0 else (cut, count - cut)
            came = pl.ds(pl.multiple_of(lax.rem(x + (NX - d), NX) * na, 128), na)
            where = x_all.at[pl.ds(ROWS * j + low, size), came]
            f = remote(where, where, xf_send.at[j, i], xf_recv.at[j, i], at_x(d))
            f.start()
            gathered[j].append(f)
            sends.append(f)

    def stage_b(j):
        if j == 0:
            for cp in local:
                cp.wait()
            for cp in weights:
                cp.wait_recv()
        for cp in gathered[j]:
            cp.wait_recv()
        rows = pl.ds(j * ROWS, ROWS)

        def column(n, carry):
            cols = pl.ds(pl.multiple_of(n * 256, 256), 256)
            v = jnp.dot(x_all[rows, :], w_gu[:, cols], preferred_element_type=jnp.float32)
            gu_own[rows, cols] = v
            gu_send[rows, cols] = v.astype(jnp.bfloat16)
            return carry

        lax.fori_loop(0, 2, column, 0)
        cp = remote(gu_send.at[rows], gu_recv.at[rows], p_send.at[j], p_recv.at[j], partner)
        cp.start()
        paired[j] = cp
        sends.append(cp)

    def stage_c(j):
        paired[j].wait_recv()
        rows = pl.ds(j * ROWS, ROWS)
        m = meta[rows, :].astype(jnp.float32)
        lanes = lax.broadcasted_iota(jnp.int32, (ROWS, 128), 1)
        hidden = []
        for c in range(NCORE):
            e = z * NCORE + c
            mine = (lanes == e) | (lanes == e + 32)
            weight = jnp.sum(jnp.where(mine, m, 0.0), axis=1, keepdims=True)
            gcols = slice(c * FFS, (c + 1) * FFS)
            ucols = slice((NCORE + c) * FFS, (NCORE + c + 1) * FFS)
            g = gu_own[rows, gcols] + gu_recv[rows, gcols].astype(jnp.float32)
            u = gu_own[rows, ucols] + gu_recv[rows, ucols].astype(jnp.float32)
            h = (0.5 * g) * (1.0 + jnp.tanh(0.5 * g)) * u * weight
            hidden.append(h.astype(jnp.bfloat16))
        hidden = jnp.concatenate(hidden, axis=1)
        def quarter(q, carry):
            v = jnp.dot(
                hidden, w_d[:, pl.ds(pl.multiple_of(q * QUART, 128), QUART)],
                preferred_element_type=jnp.float32,
            )
            part[q, rows, :] = v.astype(jnp.bfloat16)
            return carry

        lax.fori_loop(0, NX, quarter, 0)
        low, high = pl.ds(j * ROWS, CUT), pl.ds(j * ROWS + CUT, ROWS - CUT)
        cps = []
        for i, (d, q, half, slot) in enumerate(
            ((1, x2, low, 2), (3, x2, high, 3), (1, x1, high, 0), (3, x3, low, 1))
        ):
            cp = remote(
                part.at[q, half], xr.at[slot, half], xr_send.at[j, i], xr_recv.at[j, i], at_x(d)
            )
            cp.start()
            cps.append(cp)
        xred[j] = cps
        sends.extend(cps)

    def stage_g(j):
        low, high = pl.ds(j * ROWS, CUT), pl.ds(j * ROWS + CUT, ROWS - CUT)
        cps = []
        for i, (d, q, half) in enumerate(((1, x1, low), (3, x3, high))):
            xred[j][i].wait_recv()
            v = part[q, half, :].astype(jnp.float32) + xr[2 + i, half, :].astype(jnp.float32)
            part[q, half, :] = v.astype(jnp.bfloat16)
            cp = remote(
                part.at[q, half], xr.at[i, half], xc_send.at[j, i], xc_recv.at[j, i], at_x(d)
            )
            cp.start()
            cps.append(cp)
        xcom[j] = cps
        sends.extend(cps)

    def stage_d(j):
        for cp in xred[j][2:] + xcom[j]:
            cp.wait_recv()
        rows = pl.ds(j * ROWS, ROWS)
        total = part[x, rows, :].astype(jnp.float32)
        for d in range(2):
            total = total + xr[d, rows, :].astype(jnp.float32)
        ys[rows, 0:QUART] = total.astype(jnp.bfloat16)
        cps = []
        for d in (2, 1, 3):
            scol = pl.multiple_of(lax.rem(yh + d, NY) * SUB, SUB)
            cp = remote(
                ys.at[rows, pl.ds(scol, SUB)], yr.at[d - 1, rows],
                yr_send.at[j, d - 1], yr_recv.at[j, d - 1], at_y(d),
            )
            cp.start()
            cps.append(cp)
        yred[j] = cps
        sends.extend(cps)

    def stage_e(j):
        for cp in yred[j]:
            cp.wait_recv()
        rows = pl.ds(j * ROWS, ROWS)
        total = ys[rows, pl.ds(pl.multiple_of(yh * SUB, SUB), SUB)].astype(jnp.float32)
        for d in range(NY - 1):
            total = total + yr[d, rows, :].astype(jnp.float32)
        zs[rows, :] = total.astype(jnp.bfloat16)
        for k in range(PER * j, PER * j + PER):
            if k != OWN:
                cp = remote(
                    zs.at[pl.ds(k * BLOCK, BLOCK)], zr.at[k],
                    zr_send.at[k], zr_recv.at[k], at_z(-OFFSETS[k]),
                )
                cp.start()
                zred[k] = cp
                sends.append(cp)

    stages = dict(A=stage_a, F=stage_f, G=stage_g, B=stage_b, C=stage_c, D=stage_d, E=stage_e)
    for name, numbers in ORDER :
        for j in numbers:
            stages[name](j)

    total = zs[own, :].astype(jnp.float32)
    for k in range(NZ - 1):
        zred[k].wait_recv()
        total = total + zr[k].astype(jnp.float32)
    fo[dp] = total.astype(jnp.bfloat16)
    last = []
    for d in range(1, NX * NY):
        cp = remote(fo.at[dp], fo.at[dp], ag_send.at[d], ag_recv.at[d], at_dp(d))
        cp.start()
        last.append(cp)
    sends += last
    for cp in last:
        cp.wait_recv()
    for b in range(NY):
        for a in range(NX):
            width = min(SUB, QUART - b * SUB)
            start = a * QUART + b * SUB
            out[:, start : start + width] = fo[b * NX + a, :, 0:width]
    for cp in sends:
        cp.wait_send()


def per_device(tokens, routes, gates, w_gate, w_up, w_down):
    total = CHUNKS * ROWS
    bf, f32 = jnp.bfloat16, jnp.float32
    dma = pltpu.SemaphoreType.DMA
    vm = pl.BlockSpec(memory_space=pltpu.VMEM)
    hbm = pl.BlockSpec(memory_space=pl.ANY)
    return pl.pallas_call(
        kernel,
        out_shape=jax.ShapeDtypeStruct((BLOCK, HALF), bf),
        in_specs=[hbm, vm, vm, hbm, hbm, hbm],
        out_specs=vm,
        scratch_shapes=[
            pltpu.VMEM((total, HALF), bf),
            pltpu.VMEM((HALF, 2 * NCORE * FFS), bf),
            pltpu.VMEM((NCORE * FFS, HALF), bf),
            pltpu.VMEM((total, 128), bf),
            pltpu.VMEM((total, 2 * NCORE * FFS), f32),
            pltpu.VMEM((total, 2 * NCORE * FFS), bf),
            pltpu.VMEM((total, 2 * NCORE * FFS), bf),
            pltpu.VMEM((NX, total, QUART), bf),
            pltpu.VMEM((NX, total, QUART), bf),
            pltpu.VMEM((total, NY * SUB), bf),
            pltpu.VMEM((NY - 1, total, SUB), bf),
            pltpu.VMEM((total, SUB), bf),
            pltpu.VMEM((NZ, BLOCK, SUB), bf),
            pltpu.VMEM((NX * NY, BLOCK, SUB), bf),
            dma((4,)), dma((3,)), dma((3,)),
            dma((NZ,)), dma((NZ,)), dma((NZ,)), dma((NZ,)),
            dma((NZ,)), dma((NZ,)),
            dma((CHUNKS, NX - 1)), dma((CHUNKS, NX - 1)),
            dma((CHUNKS, 2)), dma((CHUNKS, 2)),
            dma((CHUNKS, NY - 1)), dma((CHUNKS, NY - 1)),
            dma((CHUNKS,)), dma((CHUNKS,)),
            dma((CHUNKS, 4)), dma((CHUNKS, 4)),
            dma((CHUNKS, 2)), dma((CHUNKS, 2)),
            dma((CHUNKS, NY - 1)), dma((CHUNKS, NY - 1)),
            dma((NZ,)), dma((NZ,)),
            dma((NX * NY,)), dma((NX * NY,)),
        ],
        compiler_params=pltpu.CompilerParams(
            collective_id=0, has_side_effects=True, vmem_limit_bytes=60 << 20
        ),
        cost_estimate=pl.CostEstimate(flops=2 * 3 * 512 * 3584 * 256, bytes_accessed=4 << 20, transcendentals=512 * 256),
    )(tokens, routes, gates, w_gate, w_up, w_down)


def solution(mesh):
    placed = (
        P("expert", "pair"),
        P("expert", None),
        P("expert", None),
        P("expert", "pair", "dp"),
        P("expert", "pair", "dp"),
        P("expert", "dp", "pair"),
    )
    return jax.shard_map(
        per_device, mesh=mesh, in_specs=placed, out_specs=P("expert", "pair"), check_vma=False
    )
```

time: 519 us -> 114 us (0.22)
  the two profiles are of different devices: /device:TPU:30 before, /device:TPU:2 now
where the time goes in v1:
time: 114 us; the launch traced here: 113 us
  Pallas kernels  110 us (96%)
  local copies, waits for them, and re-layouts  3.7 us (3%)
    pallas_call x1, Pallas kernels, per_device(): pl.pallas_call(kernel, out_shape=jax.ShapeDtypeStruct((BLOCK, HALF), bf),...  110 us
    unnamed x5, local copies, waits for them, and re-layouts  3.7 us

profile of v1, /device:TPU:2, one launch (start us, length us, event | category | flops | bytes accessed | tf_op | source)
XLA Modules:
  0.0 113.4 jit_solution(4504548100997093669)
XLA Ops:
  0.0 0.0 copy-start
  0.0 1.4 %copy.7.routes = s32[32,8]{1,0:T(8,128)} copy(s32[32,8]{0,1:T(8,128)} %param.7) | data formatting | bytes 2048 | tf_op args[1]
  1.4 0.0 copy-done
  1.4 0.7 copy.8.gates
  2.1 109.7 %shard_map.64 = bf16[32,3584]{1,0:T(8,128)(2,1)} custom-call(bf16[32,3584]{1,0:T(8,128)(2,1)} %tok.1, s32[32,8]{1,0:T(8,128)} %copy.7.routes, f32[32,8]{1,0:T(8,128)} %copy.8.gates, bf16[1,3584,128]{2,1,0:T(8,128)(2,1)} %wg.1, bf16[1,3584,128]{2,1,0:T(8,128)(2,1)} %wu.1, bf16[1,128,3584]{2,1,0:T(8,128)(2,1)} %wd.1), custom_call_target="tpu_custom_call" | custom-call | flops 2818572288 | bytes 4194304 | tf_op jit(solution)/shard_map/pallas_call | solution.py:333
  111.7 1.6 %copy.10 = bf16[32,3584]{1,0:T(8,128)(2,1)} copy(bf16[32,3584]{1,0:T(8,128)(2,1)} %shard_map.64) | data formatting | bytes 458752
Async XLA Ops:
  0.0 1.4 %copy-start = (f32[32,8]{0,1:T(8,128)S(1)}, f32[32,8]{0,1:T(8,128)}, u32[]{:S(2)}) copy-start(f32[32,8]{0,1:T(8,128)} %param.8) | copy-start | bytes 3076

commit v2 on v1

--- a/solution.py
+++ b/solution.py
@@ -15,21 +15,28 @@
 QUART = 896
 SUB = 256
 FFS = 128
-CHUNKS = 8
-PER = 2
-CUT = 32
+STARTS = (0, 2, 4, 6, 8, 10, 12, 14, 15, 16)
+CHUNKS = 9
+ALONE = CHUNKS - 1
 NB = 2
-ROWS = PER * BLOCK
+TOTAL = 512
 OFFSETS = (1, -1, 2, -2, 3, -3, 4, -4, 5, -5, 6, -6, 7, -7, 8, 0)
 OWN = NZ - 1
 JUMP = 2
 TOPK = 8
-ORDER = (('A', (0,)), ('A', (1,)), ('F', (0,)), ('A', (2,)), ('F', (1,)), ('A', (3,)), ('B', (0,)), ('F', (2,)), ('A', (4,)), ('B', (1,)), ('A', (5,)), ('F', (3,)), ('C', (0,)), ('B', (2,)), ('A', (6,)), ('F', (4,)), ('C', (1,)), ('A', (7,)), ('F', (5,)), ('B', (3,)), ('G', (0,)), ('C', (2,)), ('F', (6,)), ('B', (4,)), ('C', (3,)), ('G', (1,)), ('F', (7,)), ('B', (5,)), ('D', (0,)), ('C', (4,)), ('G', (2,)), ('B', (6,)), ('C', (5,)), ('G', (3,)), ('D', (1,)), ('E', (0,)), ('B', (7,)), ('C', (6,)), ('G', (4,)), ('D', (2,)), ('E', (1,)), ('G', (5,)), ('C', (7,)), ('D', (3,)), ('G', (6,)), ('E', (2,)), ('D', (4,)), ('D', (5,)), ('G', (7,)), ('E', (3,)), ('D', (6,)), ('E', (4,)), ('D', (7,)), ('E', (5,)), ('E', (6,)), ('E', (7,)))
+ORDER = (
+    ("A", 0), ("A", 1), ("F", 0), ("A", 2), ("F", 1), ("A", 3), ("B", 0), ("F", 2), ("B", 1), ("A", 4), ("F", 3), ("A", 5),
+    ("B", 2), ("C", 0), ("F", 4), ("C", 1), ("A", 6), ("A", 7), ("F", 5), ("B", 3), ("G", 0), ("C", 2), ("B", 4), ("G", 1),
+    ("F", 6), ("C", 3), ("F", 7), ("D", 0), ("B", 5), ("G", 2), ("C", 4), ("D", 1), ("B", 6), ("G", 3), ("E", 0), ("C", 5),
+    ("D", 2), ("B", 7), ("G", 4), ("E", 1), ("D", 3), ("C", 6), ("G", 5), ("E", 2), ("D", 4), ("C", 7), ("B", 8), ("E", 3),
+    ("G", 6), ("D", 5), ("G", 7), ("E", 4), ("C", 8), ("D", 6), ("D", 7), ("E", 5), ("G", 8), ("E", 6), ("E", 7), ("D", 8),
+    ("E", 8),
+)
 
 
 def kernel(
     tok, routes, gates, wg, wu, wd, out,
-    x_all, w_gu, w_d, meta, gu_own, gu_send, gu_recv, part, xr, ys, yr, zs, zr, fo,
+    x_all, w_gu, w_d, meta, gu_own, gu_send, gu_recv, part, xr, ys, yr, zs, zr, fo, flat,
     w_loc, w_send, w_recv, zg_send, zg_recv, mg_send, mg_recv, bg_send, bg_recv, xg_send, xg_recv,
     xf_send, xf_recv, yg_send, yg_recv,
     p_send, p_recv, xr_send, xr_recv, xc_send, xc_recv, yr_send, yr_recv, zr_send, zr_recv, ag_send, ag_recv,
@@ -85,17 +92,21 @@
     for cp in local:
         cp.start()
 
-    lane = lax.broadcasted_iota(jnp.int32, (BLOCK, 128), 1)
+    flat[...] = jnp.zeros((2 * TOPK, 128), jnp.float32)
+    flat[0:TOPK, 0:BLOCK] = routes[...].astype(jnp.float32)
+    flat[TOPK:, 0:BLOCK] = gates[...]
+    table = jnp.transpose(flat[...])[0:BLOCK]
+    lane = lax.broadcasted_iota(jnp.int32, (BLOCK, 128), 1).astype(jnp.float32)
     first = jnp.zeros((BLOCK, 128), jnp.float32)
     second = jnp.zeros((BLOCK, 128), jnp.float32)
     for k in range(TOPK):
-        r = routes[:, k : k + 1]
-        g = gates[:, k : k + 1]
+        r = table[:, k : k + 1]
+        g = table[:, TOPK + k : TOPK + k + 1]
         first = first + jnp.where(lane == r, g, 0.0)
-        second = second + jnp.where(lane == r + 32, g, 0.0)
+        second = second + jnp.where(lane == r + 32.0, g, 0.0)
     low = second - second.astype(jnp.bfloat16).astype(jnp.float32)
     meta[own, :] = jnp.where(lane < 32, first, low).astype(jnp.bfloat16)
-    ys[:, QUART:] = jnp.zeros((CHUNKS * ROWS, NY * SUB - QUART), jnp.bfloat16)
+    ys[:, QUART:] = jnp.zeros((TOTAL, NY * SUB - QUART), jnp.bfloat16)
 
     mine_in.wait()
     pl.semaphore_wait(barrier, NZ - 1 + NX * NY - 1 + 2)
@@ -133,7 +144,8 @@
         cp.start()
     sends += weights
 
-    gathered = {}
+    gathered = {ALONE: []}
+    loaded = []
     halves = {}
     paired = {}
     xred = {}
@@ -141,16 +153,20 @@
     yred = {}
     zred = {}
 
+    def span(j):
+        return pl.ds(STARTS[j] * BLOCK, (STARTS[j + 1] - STARTS[j]) * BLOCK)
+
+    def split(j):
+        low, count = STARTS[j] * BLOCK, (STARTS[j + 1] - STARTS[j]) * BLOCK // 2
+        return pl.ds(low, count), pl.ds(low + count, count)
+
     def stage_a(j):
-        for k in range(PER * j, PER * j + PER):
-            if k == OWN:
-                continue
+        for k in range(STARTS[j], STARTS[j + 1]):
             for cp in zgot[k]:
                 cp.wait_recv()
             if k + 2 * JUMP < OWN:
                 hop(k, k + 2 * JUMP)
-        count = ROWS - BLOCK if j == CHUNKS - 1 else ROWS
-        rows = pl.ds(ROWS * j, count)
+        rows = span(j)
         where = x_all.at[rows, acol]
         cps = [
             remote(where, where, xg_send.at[j, d - 1], xg_recv.at[j, d - 1], at_x(d))
@@ -170,27 +186,25 @@
         sends.extend(cps + ycps)
 
     def stage_f(j):
-        count = ROWS - BLOCK if j == CHUNKS - 1 else ROWS
-        cut = count // 2
         for i, (cp, d) in enumerate(zip(halves[j], (1, 3))):
             cp.wait_recv()
-            low, size = (0, cut) if i == 0 else (cut, count - cut)
             came = pl.ds(pl.multiple_of(lax.rem(x + (NX - d), NX) * na, 128), na)
-            where = x_all.at[pl.ds(ROWS * j + low, size), came]
+            where = x_all.at[split(j)[i], came]
             f = remote(where, where, xf_send.at[j, i], xf_recv.at[j, i], at_x(d))
             f.start()
             gathered[j].append(f)
             sends.append(f)
 
     def stage_b(j):
-        if j == 0:
+        if not loaded:
+            loaded.append(j)
             for cp in local:
                 cp.wait()
             for cp in weights:
                 cp.wait_recv()
         for cp in gathered[j]:
             cp.wait_recv()
-        rows = pl.ds(j * ROWS, ROWS)
+        rows = span(j)
 
         def column(n, carry):
             cols = pl.ds(pl.multiple_of(n * 256, 256), 256)
@@ -207,9 +221,9 @@
 
     def stage_c(j):
         paired[j].wait_recv()
-        rows = pl.ds(j * ROWS, ROWS)
+        rows = span(j)
         m = meta[rows, :].astype(jnp.float32)
-        lanes = lax.broadcasted_iota(jnp.int32, (ROWS, 128), 1)
+        lanes = lax.broadcasted_iota(jnp.int32, m.shape, 1)
         hidden = []
         for c in range(NCORE):
             e = z * NCORE + c
@@ -231,7 +245,7 @@
             return carry
 
         lax.fori_loop(0, NX, quarter, 0)
-        low, high = pl.ds(j * ROWS, CUT), pl.ds(j * ROWS + CUT, ROWS - CUT)
+        low, high = split(j)
         cps = []
         for i, (d, q, half, slot) in enumerate(
             ((1, x2, low, 2), (3, x2, high, 3), (1, x1, high, 0), (3, x3, low, 1))
@@ -245,7 +259,7 @@
         sends.extend(cps)
 
     def stage_g(j):
-        low, high = pl.ds(j * ROWS, CUT), pl.ds(j * ROWS + CUT, ROWS - CUT)
+        low, high = split(j)
         cps = []
         for i, (d, q, half) in enumerate(((1, x1, low), (3, x3, high))):
             xred[j][i].wait_recv()
@@ -262,7 +276,7 @@
     def stage_d(j):
         for cp in xred[j][2:] + xcom[j]:
             cp.wait_recv()
-        rows = pl.ds(j * ROWS, ROWS)
+        rows = span(j)
         total = part[x, rows, :].astype(jnp.float32)
         for d in range(2):
             total = total + xr[d, rows, :].astype(jnp.float32)
@@ -282,12 +296,12 @@
     def stage_e(j):
         for cp in yred[j]:
             cp.wait_recv()
-        rows = pl.ds(j * ROWS, ROWS)
+        rows = span(j)
         total = ys[rows, pl.ds(pl.multiple_of(yh * SUB, SUB), SUB)].astype(jnp.float32)
         for d in range(NY - 1):
             total = total + yr[d, rows, :].astype(jnp.float32)
         zs[rows, :] = total.astype(jnp.bfloat16)
-        for k in range(PER * j, PER * j + PER):
+        for k in range(STARTS[j], STARTS[j + 1]):
             if k != OWN:
                 cp = remote(
                     zs.at[pl.ds(k * BLOCK, BLOCK)], zr.at[k],
@@ -298,9 +312,8 @@
                 sends.append(cp)
 
     stages = dict(A=stage_a, F=stage_f, G=stage_g, B=stage_b, C=stage_c, D=stage_d, E=stage_e)
-    for name, numbers in ORDER :
-        for j in numbers:
-            stages[name](j)
+    for name, j in ORDER:
+        stages[name](j)
 
     total = zs[own, :].astype(jnp.float32)
     for k in range(NZ - 1):
@@ -325,7 +338,7 @@
 
 
 def per_device(tokens, routes, gates, w_gate, w_up, w_down):
-    total = CHUNKS * ROWS
+    total = TOTAL
     bf, f32 = jnp.bfloat16, jnp.float32
     dma = pltpu.SemaphoreType.DMA
     vm = pl.BlockSpec(memory_space=pltpu.VMEM)
@@ -350,6 +363,7 @@
             pltpu.VMEM((total, SUB), bf),
             pltpu.VMEM((NZ, BLOCK, SUB), bf),
             pltpu.VMEM((NX * NY, BLOCK, SUB), bf),
+            pltpu.VMEM((2 * TOPK, 128), f32),
             dma((4,)), dma((3,)), dma((3,)),
             dma((NZ,)), dma((NZ,)), dma((NZ,)), dma((NZ,)),
             dma((NZ,)), dma((NZ,)),
@@ -367,7 +381,7 @@
             collective_id=0, has_side_effects=True, vmem_limit_bytes=60 << 20
         ),
         cost_estimate=pl.CostEstimate(flops=2 * 3 * 512 * 3584 * 256, bytes_accessed=4 << 20, transcendentals=512 * 256),
-    )(tokens, routes, gates, w_gate, w_up, w_down)
+    )(tokens, routes.T, gates.T, w_gate, w_up, w_down)
 
 
 def solution(mesh):

time: 114 us -> 113 us (level)
  the two profiles are of different devices: /device:TPU:2 before, /device:TPU:70 now
where the time goes in v2:
time: 113 us
  Pallas kernels  111 us (98%)
  local copies, waits for them, and re-layouts  1.64 us (1%)
    pallas_call x1, Pallas kernels, per_device(): pl.pallas_call(kernel, out_shape=jax.ShapeDtypeStruct((BLOCK, HALF), bf),...  111 us

profile of v2, /device:TPU:70, one launch (start us, length us, event | category | flops | bytes accessed | tf_op | source)
XLA Modules:
  0.0 112.7 jit_solution(3798211098005697840)
XLA Ops:
  0.0 111.0 %shard_map.64 = bf16[32,3584]{1,0:T(8,128)(2,1)} custom-call(bf16[32,3584]{1,0:T(8,128)(2,1)} %tok.1, s32[8,32]{1,0:T(8,128)} %bitcast.2, f32[8,32]{1,0:T(8,128)} %bitcast.3, bf16[1,3584,128]{2,1,0:T(8,128)(2,1)} %wg.1, bf16[1,3584,128]{2,1,0:T(8,128)(2,1)} %wu.1, bf16[1,128,3584]{2,1,0:T(8,128)(2,1)} %wd.1), custom_call_target="tpu_custom_call" | custom-call | flops 2818572288 | bytes 4194304 | tf_op jit(solution)/shard_map/pallas_call | solution.py:346
  111.0 1.6 %copy.8 = bf16[32,3584]{1,0:T(8,128)(2,1)} copy(bf16[32,3584]{1,0:T(8,128)(2,1)} %shard_map.64) | data formatting | bytes 458752

commit v3 on v2

--- a/solution.py
+++ b/solution.py
@@ -71,10 +71,10 @@
         )
 
     barrier = pltpu.get_barrier_semaphore()
-    for k in range(NZ - 1):
-        pl.semaphore_signal(barrier, inc=1, device_id=at_z(OFFSETS[k]), device_id_type=MESH)
-    for d in range(1, NX * NY):
-        pl.semaphore_signal(barrier, inc=1, device_id=at_dp(d), device_id_type=MESH)
+    near = [at_z(off) for off in OFFSETS[: 2 * JUMP]]
+    near += [at_x(d) for d in range(1, NX)] + [at_y(d) for d in range(1, NY)]
+    for where in near:
+        pl.semaphore_signal(barrier, inc=1, device_id=where, device_id_type=MESH)
     pl.semaphore_signal(barrier, inc=1, device_id=sibling, device_id_type=MESH)
     pl.semaphore_signal(barrier, inc=1, device_id=partner, device_id_type=MESH)
 
@@ -109,7 +109,7 @@
     ys[:, QUART:] = jnp.zeros((TOTAL, NY * SUB - QUART), jnp.bfloat16)
 
     mine_in.wait()
-    pl.semaphore_wait(barrier, NZ - 1 + NX * NY - 1 + 2)
+    pl.semaphore_wait(barrier, len(near) + 2)
 
     nb = NB * 128
     na = QUART - nb

time: 113 us -> 108 us (0.956)
  the two profiles are of different devices: /device:TPU:70 before, /device:TPU:16 now
where the time goes in v3:
time: 108 us
  Pallas kernels  106 us (98%)
  local copies, waits for them, and re-layouts  1.64 us (2%)
    pallas_call x1, Pallas kernels, per_device(): pl.pallas_call(kernel, out_shape=jax.ShapeDtypeStruct((BLOCK, HALF), bf),...  106 us

profile of v3, /device:TPU:16, one launch (start us, length us, event | category | flops | bytes accessed | tf_op | source)
XLA Modules:
  0.0 107.6 jit_solution(15160726501126767424)
XLA Ops:
  0.0 105.9 %shard_map.64 = bf16[32,3584]{1,0:T(8,128)(2,1)} custom-call(bf16[32,3584]{1,0:T(8,128)(2,1)} %tok.1, s32[8,32]{1,0:T(8,128)} %bitcast.2, f32[8,32]{1,0:T(8,128)} %bitcast.3, bf16[1,3584,128]{2,1,0:T(8,128)(2,1)} %wg.1, bf16[1,3584,128]{2,1,0:T(8,128)(2,1)} %wu.1, bf16[1,128,3584]{2,1,0:T(8,128)(2,1)} %wd.1), custom_call_target="tpu_custom_call" | custom-call | flops 2818572288 | bytes 4194304 | tf_op jit(solution)/shard_map/pallas_call | solution.py:346
  105.9 1.6 %copy.8 = bf16[32,3584]{1,0:T(8,128)(2,1)} copy(bf16[32,3584]{1,0:T(8,128)(2,1)} %shard_map.64) | data formatting | bytes 458752
